TPU v7x, 128 devices: a whole 4x4x4 slice. The times are simulated.
128 devices in a mesh: sky: 8 (over x, core), det: 16 (over z, y).
Axes of the slice: x: 4, y: 4, z: 4, core: 2. Of those that a mesh axis runs over, the one named last changes fastest.
Arguments:
- templates: bfloat16 [256, 512, 512], P(('sky', 'det')), may hold values from -6 to 6
- science: bfloat16 [256, 512, 512], P(('sky', 'det')), may hold values from -6 to 6
- intersection: int32 [256, 4], P(('sky', 'det')), may hold values from 0 to 63, as said below
- row_warp: int32 [256, 4], P(('sky', 'det')), may hold values from 0 to 7
- col_warp: int32 [256, 4], P(('sky', 'det')), may hold values from 0 to 7
- warps: bfloat16 [8, 512, 512], replicated, may hold values from -0.25 to 0.25
- taps: float32 [16, 21], replicated, may hold values from -1.25 to 1.25
- basis_row: int32 [256, 5], P(('sky', 'det')), may hold values from 0 to 15
- basis_col: int32 [256, 5], P(('sky', 'det')), may hold values from 0 to 15
- coef: float32 [256, 5, 3], P(('sky', 'det')), may hold values from -4 to 4
- home: int32 [256], P(('sky', 'det')), may hold values from 0 to 31, as said below
Outputs:
- returned: bfloat16 [4096, 512, 512], P(('sky', 'det'))
Inputs may be any that keep to these rules, and one draw needn't show every extreme that they name: `intersection`: among the 8 entries q of one device's detector tiles, at most 2 share a value of (q // 2) % 16, and 2 is reached by some value in every such group. `home`: the 2 values of one device's detector tiles are distinct and share one value of home // 2, so both difference tiles of a device go to the same det index.
All inputs are finite; a program needn't handle non-finite values.
Results may differ from a plain program's by a relative error of at most 0.019.
Values may be sent and summed in bfloat16 or wider, within the bound.
No kernel may reach another device: no remote copies, remote signals or barrier semaphores. Data moves between devices by JAX's collectives and lax.ppermute only.
A program may use at most 192 MiB of HBM per device.

v0:
```python
import jax
import jax.numpy as jnp
from jax import lax
from jax.sharding import PartitionSpec as P

SIDE = 512


def passed_along(block, axis, distance):
    devices = range(lax.axis_size(axis))
    route = [((i - distance) % len(devices), i) for i in devices]
    return lax.ppermute(block, axis, route)


def make_bands(taps):
    width = taps.shape[1]
    offsets = jnp.arange(SIDE)[None, :] - jnp.arange(SIDE)[:, None] + width // 2
    selector = (jnp.arange(width)[:, None, None] == offsets[None]).astype(jnp.float32)
    bands = jnp.einsum("tij,ft->fij", selector, taps, precision=lax.Precision.HIGHEST)
    return bands.astype(jnp.bfloat16)


def warp_tiles(tiles, row_index, col_index, warps):
    count = tiles.shape[0]
    groups = count // 8

    def warp_group(items):
        group_tiles, group_rows, group_cols = items
        left = jnp.take(warps, group_rows, axis=0)
        right = jnp.take(warps, group_cols, axis=0)
        inner = jnp.einsum(
            "nij,njk->nik", left, group_tiles, preferred_element_type=jnp.float32
        ).astype(jnp.bfloat16)
        return jnp.einsum("nik,nlk->nil", inner, right, preferred_element_type=jnp.float32).astype(
            jnp.bfloat16
        )

    pieces = lax.map(
        warp_group,
        (
            tiles.reshape(groups, 8, SIDE, SIDE),
            row_index.reshape(groups, 8),
            col_index.reshape(groups, 8),
        ),
    )
    return pieces.reshape(count, SIDE, SIDE)


def shards(
    templates,
    science,
    intersection,
    row_warp,
    col_warp,
    warps,
    taps,
    basis_row,
    basis_col,
    coef,
    home,
):
    tpl_count = templates.shape[0]
    tgt_count = science.shape[0]
    per_tile = intersection.shape[1]
    det_count = lax.axis_size("det")
    limit = max(2, 2 * tgt_count * per_tile // det_count)
    limit_back = max(2, 2 * tgt_count // det_count)
    following = passed_along(templates, "sky", -1)
    candidates = jnp.concatenate([templates, following], axis=0)
    flat = intersection.reshape(-1)
    owner = flat // tpl_count % det_count
    local = flat // (det_count * tpl_count) * tpl_count + flat % tpl_count
    onehot = (owner[:, None] == jnp.arange(det_count)[None, :]).astype(jnp.int32)
    earlier = jnp.cumsum(onehot, axis=0) - onehot
    position = owner * limit + jnp.sum(earlier * onehot, axis=1)
    table = jnp.full((det_count * limit,), -1, jnp.int32).at[position].set(local)
    flat_rows = row_warp.reshape(-1)
    flat_cols = col_warp.reshape(-1)
    row_table = jnp.zeros((det_count * limit,), jnp.int32).at[position].set(flat_rows)
    col_table = jnp.zeros((det_count * limit,), jnp.int32).at[position].set(flat_cols)
    wanted, wanted_rows, wanted_cols = (
        lax.all_to_all(table, "det", split_axis=0, concat_axis=0, tiled=True),
        lax.all_to_all(row_table, "det", split_axis=0, concat_axis=0, tiled=True),
        lax.all_to_all(col_table, "det", split_axis=0, concat_axis=0, tiled=True),
    )
    live = (wanted >= 0).astype(jnp.bfloat16)
    outgoing = jnp.take(candidates, jnp.maximum(wanted, 0), axis=0)
    pieces = warp_tiles(outgoing, wanted_rows, wanted_cols, warps) * live[:, None, None]
    arrived = lax.all_to_all(pieces, "det", split_axis=0, concat_axis=0, tiled=True)
    mine = jnp.take(arrived, position, axis=0)
    warped = jnp.sum(
        mine.reshape(tgt_count, per_tile, SIDE, SIDE).astype(jnp.float32), axis=1
    ).astype(jnp.bfloat16)
    bands = make_bands(taps)
    coord = (2.0 * jnp.arange(SIDE, dtype=jnp.float32) + 1.0) / SIDE - 1.0

    def match_tile(items):
        tile, sci, row_pick, col_pick, factors = items
        rowband = jnp.take(bands, row_pick, axis=0)
        colband = jnp.take(bands, col_pick, axis=0)
        half = jnp.einsum("bij,jk->bik", rowband, tile, preferred_element_type=jnp.float32).astype(
            jnp.bfloat16
        )
        conv = jnp.einsum("bik,blk->bil", half, colband, preferred_element_type=jnp.float32)
        field = (
            factors[:, 0, None, None]
            + factors[:, 1, None, None] * coord[None, :, None]
            + factors[:, 2, None, None] * coord[None, None, :]
        )
        model = jnp.sum(field * conv, axis=0)
        return (sci.astype(jnp.float32) - model).astype(jnp.bfloat16)

    diffs = lax.map(match_tile, (warped, science, basis_row, basis_col, coef))
    outgoing_back = (
        jnp.zeros((det_count * limit_back, SIDE, SIDE), jnp.bfloat16).at[home].set(diffs)
    )
    return lax.all_to_all(outgoing_back, "det", split_axis=0, concat_axis=0, tiled=True)


def solution(mesh):
    placed = (
        P(("sky", "det"), None, None),
        P(("sky", "det"), None, None),
        P(("sky", "det"), None),
        P(("sky", "det"), None),
        P(("sky", "det"), None),
        P(),
        P(),
        P(("sky", "det"), None),
        P(("sky", "det"), None),
        P(("sky", "det"), None, None),
        P(("sky", "det")),
    )
    return jax.shard_map(
        shards, mesh=mesh, in_specs=placed, out_specs=P(("sky", "det"), None, None), check_vma=False
    )
```

profile of v0, /device:TPU:2, one launch (start us, length us, event | category | flops | bytes accessed | tf_op | source)
XLA Modules:
  0.0 663.5 jit_solution(16720198550645768071)
XLA Ops:
  0.0 0.8 reshape.315
  0.8 0.8 reshape.316
  3.2 8.0 %all-to-all-start.1 = ((s32[16,2,1]{1,2,0:T(1,128)}), s32[16,2,1]{1,2,0:T(1,128)S(1)}, u32[]{:S(2)}, u32[]{:S(2)}) async-start(s32[16,2,1]{1,2,0:T(1,128)} %bitcast.9), calls=%async_computation.1 | async-start | bytes 16384 | tf_op jit(solution)/shard_map/all_to_all | solution.py:82
  11.2 0.8 reshape.375
  13.3 0.8 reshape.391
  15.3 3.3 all-to-all-done.1
  18.6 3.9 all-to-all-start
  22.8 7.3 %all-to-all-done = s32[16,2,1]{1,2,0:T(1,128)S(1)} async-done(((s32[16,2,1]{1,2,0:T(1,128)}), s32[16,2,1]{1,2,0:T(1,128)S(1)}, u32[]{:S(2)}, u32[]{:S(2)}) %all-to-all-start) | async-done | bytes 160 | tf_op jit(solution)/shard_map/all_to_all | solution.py:83
  30.1 3.4 all-to-all-start.2
  34.1 0.7 reduce.15
  34.9 6.1 all-to-all-done.2
  41.0 0.7 reduce.16
  42.0 1.4 pad_maximum_fusion
  43.4 7.1 %gather_fusion.4 = bf16[32,512,512]{2,1,0:T(8,128)(2,1)} fusion(bf16[4,512,512]{2,1,0:T(8,128)(2,1)S(1)} %pad_maximum_fusion, s32[1024]{0:T(1024)S(1)} %pad_clamp_fusion.5), kind=kCustom, calls=%fused_computation.4 | custom fusion | bytes 33554560 | tf_op jit(solution)/shard_map/jit(_take)/gather | solution.py:87
  50.4 14.1 %broadcast_select_fusion = bf16[4,8,512,512]{3,2,1,0:T(8,128)(2,1)} fusion(bf16[4,8,512,512]{3,2,1,0:T(8,128)(2,1)} %bitcast.82, pred[4,8]{1,0:T(4,128)(4,1)S(1)} %le.34), kind=kLoop, calls=%fused_computation.71 | loop fusion | flops 8388608 | bytes 33554464 | tf_op jit(solution)/shard_map/jit(_take)/select_n | solution.py:87
  64.6 84.7 %while.22 = (s32[]{:T(128)}, bf16[4,8,512,512]{3,2,1,0:T(8,128)(2,1)}, s32[4,8]{1,0:T(4,128)S(1)}, bf16[8,512,512]{2,1,0:T(8,128)(2,1)}, bf16[4,8,512,512]{3,2,1,0:T(8,128)(2,1)}, /*index=5*/s32[4,8]{1,0:T(4,128)S(1)}, s32[]{:T(128)}) while((s32[]{:T(128)}, bf16[4,8,512,512]{3,2,1,0:T(8,128)(2,1)}, s32[4,8]{1,0:T(4,128)S(1)}, ...), condition=%wide.region_6.8_spmd, body=%wide.region_5.7_spmd.sunk | while | flops 4303357952 | bytes 33564016 | solution.py:38
  64.6 4.9 gather_fusion
  69.5 5.0 gather_fusion.1
  74.5 11.2 %bitcast_dynamic-update-slice_fusion.2 = bf16[4,8,512,512]{3,2,1,0:T(8,128)(2,1)} fusion(bf16[4,8,512,512]{3,2,1,0:T(8,128)(2,1)} %get-tuple-element.330, s32[]{:T(128)} %get-tuple-element.329, bf16[8,512,512]{2,1,0:T(8,128)(2,1)} %gather_fusion, pred[8]{0:T(512)(128)(4,1)S(1)} %get-tuple-element.302, bf16[8,512,512]{2,1,0:T(8,128)(2,1)} %gather_fusion.1, ...), kind=kOutput, calls=%fused_computation.11.clone.1 | convolution fusion | flops 4303355904 | bytes 16778256 | tf_op jit(solution)/shard_map/while/body/eval_jaxpr/nik,nlk->nil/dot_general | solution.py:34
  85.8 4.9 gather_fusion
  90.7 5.0 gather_fusion.1
  95.7 11.2 %bitcast_dynamic-update-slice_fusion.2 = bf16[4,8,512,512]{3,2,1,0:T(8,128)(2,1)} fusion(bf16[4,8,512,512]{3,2,1,0:T(8,128)(2,1)} %get-tuple-element.330, s32[]{:T(128)} %get-tuple-element.329, bf16[8,512,512]{2,1,0:T(8,128)(2,1)} %gather_fusion, pred[8]{0:T(512)(128)(4,1)S(1)} %get-tuple-element.302, bf16[8,512,512]{2,1,0:T(8,128)(2,1)} %gather_fusion.1, ...), kind=kOutput, calls=%fused_computation.11.clone.1 | convolution fusion | flops 4303355904 | bytes 16778256 | tf_op jit(solution)/shard_map/while/body/eval_jaxpr/nik,nlk->nil/dot_general | solution.py:34
  106.9 4.9 gather_fusion
  111.9 5.0 gather_fusion.1
  116.8 11.2 %bitcast_dynamic-update-slice_fusion.2 = bf16[4,8,512,512]{3,2,1,0:T(8,128)(2,1)} fusion(bf16[4,8,512,512]{3,2,1,0:T(8,128)(2,1)} %get-tuple-element.330, s32[]{:T(128)} %get-tuple-element.329, bf16[8,512,512]{2,1,0:T(8,128)(2,1)} %gather_fusion, pred[8]{0:T(512)(128)(4,1)S(1)} %get-tuple-element.302, bf16[8,512,512]{2,1,0:T(8,128)(2,1)} %gather_fusion.1, ...), kind=kOutput, calls=%fused_computation.11.clone.1 | convolution fusion | flops 4303355904 | bytes 16778256 | tf_op jit(solution)/shard_map/while/body/eval_jaxpr/nik,nlk->nil/dot_general | solution.py:34
  128.1 4.9 gather_fusion
  133.0 5.0 gather_fusion.1
  138.0 11.2 %bitcast_dynamic-update-slice_fusion.2 = bf16[4,8,512,512]{3,2,1,0:T(8,128)(2,1)} fusion(bf16[4,8,512,512]{3,2,1,0:T(8,128)(2,1)} %get-tuple-element.330, s32[]{:T(128)} %get-tuple-element.329, bf16[8,512,512]{2,1,0:T(8,128)(2,1)} %gather_fusion, pred[8]{0:T(512)(128)(4,1)S(1)} %get-tuple-element.302, bf16[8,512,512]{2,1,0:T(8,128)(2,1)} %gather_fusion.1, ...), kind=kOutput, calls=%fused_computation.11.clone.1 | convolution fusion | flops 4303355904 | bytes 16778256 | tf_op jit(solution)/shard_map/while/body/eval_jaxpr/nik,nlk->nil/dot_general | solution.py:34
  149.2 14.0 %bitcast_multiply_fusion = bf16[32,512,512]{2,1,0:T(8,128)(2,1)} fusion(bf16[4,8,512,512]{3,2,1,0:T(8,128)(2,1)} %get-tuple-element.89, bf16[32]{0:T(256)(128)(2,1)S(1)} %reshape.322), kind=kLoop, calls=%fused_computation.70 | loop fusion | flops 8388608 | bytes 33554496 | tf_op jit(solution)/shard_map/mul | solution.py:88
  163.2 5.3 all-to-all-start.3
  168.8 12.8 %convert_bitcast_fusion = bf16[16,512,512]{2,0,1:T(8,128)(2,1)} fusion(s32[512,512]{1,0:T(8,128)S(1)} %subtract_add_fusion, f32[16,21]{1,0:T(8,128)S(1)} %copy-done), kind=kOutput, calls=%fused_computation.73 | convolution fusion | flops 1066663936 | bytes 9438528 | tf_op jit(solution)/shard_map/tij,ft->fij/dot_general | solution.py:19
  181.6 11.3 %copy.25 = bf16[16,512,512]{2,1,0:T(8,128)(2,1)} copy(bf16[16,512,512]{2,0,1:T(8,128)(2,1)} %convert_bitcast_fusion) | data formatting | bytes 16777216
  193.0 215.6 %all-to-all-done.3 = bf16[32,512,512]{2,1,0:T(8,128)(2,1)} async-done(((bf16[32,512,512]{2,1,0:T(8,128)(2,1)}), bf16[32,512,512]{2,1,0:T(8,128)(2,1)}, u32[]{:S(2)}, u32[]{:S(2)}) %all-to-all-start.3) | async-done | bytes 16777248 | tf_op jit(solution)/shard_map/all_to_all | solution.py:89
  408.6 8.6 %gather_fusion.5 = bf16[8,512,512]{2,1,0:T(8,128)(2,1)} fusion(bf16[32,512,512]{2,1,0:T(8,128)(2,1)} %all-to-all-done.3, s32[1024]{0:T(1024)S(1)} %pad_clamp_fusion.4), kind=kCustom, calls=%fused_computation.5 | custom fusion | bytes 8388640 | tf_op jit(solution)/shard_map/jit(_take)/gather | solution.py:90
  417.2 4.4 select_reduce_fusion
  421.7 36.9 %while.23 = (s32[]{:T(128)}, bf16[2,512,512]{2,1,0:T(8,128)(2,1)}, bf16[2,512,512]{2,1,0:T(8,128)(2,1)}, f32[2,5,3]{1,0,2:T(2,128)S(1)}, s32[2,5]{1,0:T(2,128)S(...) while((s32[]{:T(128)}, bf16[2,512,512]{2,1,0:T(8,128)(2,1)}, ...), condition=%wide.region_10.13_spmd.clone.clone, body=%wide.region_8.12_spmd.clone.clone.sunk | while | flops 2692754944 | bytes 19453628 | solution.py:113
  421.8 4.1 gather_fusion.2
  426.0 5.7 gather_fusion.3
  431.7 6.1 multiply_reduce_fusion.2
  437.8 2.3 fusion.99
  440.3 4.1 gather_fusion.2
  444.4 5.7 gather_fusion.3
  450.1 6.1 multiply_reduce_fusion.2
  456.2 2.3 fusion.99
  458.5 6.0 broadcast_in_dim.71
  464.6 2.8 scatter_fusion
  467.3 190.0 %all_to_all.37 = bf16[32,512,512]{2,1,0:T(8,128)(2,1)S(1)} all-to-all(bf16[32,512,512]{2,1,0:T(8,128)(2,1)} %scatter_fusion), channel_id=1, replica_groups=mesh['sky'=8,'det'=16] {'det'}, dimensions={0} | all-to-all | bytes 33554432 | tf_op jit(solution)/shard_map/all_to_all | solution.py:117
  657.3 6.2 copy.49
  (74 shorter events, 5.9 us)
Async XLA Ops:
  0.0 168.8 %copy-start = (f32[16,21]{1,0:T(8,128)S(1)}, f32[16,21]{1,0:T(8,128)}, u32[]{:S(2)}) copy-start(f32[16,21]{1,0:T(8,128)} %param.25) | copy-start | bytes 4036
  0.0 41.9 %collective-permute-start = (bf16[2,512,512]{2,1,0:T(8,128)(2,1)}, bf16[2,512,512]{2,1,0:T(8,128)(2,1)S(1)}, u32[]{:S(2)}, u32[]{:S(2)}) collective-permute-start(bf16[2,512,512]{2,1,0:T(8,128)(2,1)} %param.19), channel_id=1, source_target_pairs={{16,0},{32,16},{48,32},{64,48},{80,64},{96,80},{112,96},{0,112},{1... | collective-permute-start | bytes 3145736 | tf_op jit(solution)/shard_map/ppermute | solution.py:12
  3.2 15.5 %all-to-all-start.1 = ((s32[16,2,1]{1,2,0:T(1,128)}), s32[16,2,1]{1,2,0:T(1,128)S(1)}, u32[]{:S(2)}, u32[]{:S(2)}) async-start(s32[16,2,1]{1,2,0:T(1,128)} %bitcast.9), calls=%async_computation.1 | async-start | bytes 16384 | tf_op jit(solution)/shard_map/all_to_all | solution.py:82
  18.6 11.5 %all-to-all-start = ((s32[16,2,1]{1,2,0:T(1,128)}), s32[16,2,1]{1,2,0:T(1,128)S(1)}, u32[]{:S(2)}, u32[]{:S(2)}) async-start(s32[16,2,1]{1,2,0:T(1,128)} %bitcast.8), calls=%async_computation | async-start | bytes 16384 | tf_op jit(solution)/shard_map/all_to_all | solution.py:83
  30.1 10.9 %all-to-all-start.2 = ((s32[16,2,1]{1,2,0:T(1,128)}), s32[16,2,1]{1,2,0:T(1,128)S(1)}, u32[]{:S(2)}, u32[]{:S(2)}) async-start(s32[16,2,1]{1,2,0:T(1,128)} %bitcast.11), calls=%async_computation.2 | async-start | bytes 16384 | tf_op jit(solution)/shard_map/all_to_all | solution.py:84
  163.2 245.4 %all-to-all-start.3 = ((bf16[32,512,512]{2,1,0:T(8,128)(2,1)}), bf16[32,512,512]{2,1,0:T(8,128)(2,1)}, u32[]{:S(2)}, u32[]{:S(2)}) async-start(bf16[32,512,512]{2,1,0:T(8,128)(2,1)} %bitcast_multiply_fusion), calls=%async_computation.3 | async-start | bytes 33554432 | tf_op jit(solution)/shard_map/all_to_all | solution.py:89
  181.6 11.4 %copy-start.7 = (s32[2]{0:T(128)S(1)}, s32[2]{0:T(128)}, u32[]{:S(2)}) copy-start(s32[2]{0:T(128)} %param.29) | copy-start | bytes 28
  181.6 11.4 %copy-start.6 = (s32[2,4]{1,0:T(2,128)S(1)}, s32[2,4]{1,0:T(2,128)}, u32[]{:S(2)}) copy-start(s32[2,4]{1,0:T(2,128)} %param.21) | copy-start | bytes 100
  417.2 4.4 copy-start.3
  417.2 4.4 copy-start.4
  417.2 4.4 copy-start.5
  458.5 6.0 copy-start.2
  657.3 6.2 copy-start.1
where the time goes:
time: 665 us; the launch traced here: 664 us
  waiting for transfers between devices  232 us (35%)
  blocking collectives  190 us (29%)
  local copies, waits for them, and re-layouts  109 us (16%)
  matrix products  70 us (11%)
  other arithmetic  40.9 us (6%)
  starting transfers between devices  20.7 us (3%)
    all_to_all x1, waiting for transfers between devices, shards(): lax.all_to_all(pieces, 'det', split_axis=0, concat_axis=0, tiled=True)  216 us
    all_to_all x1, blocking collectives, shards(): lax.all_to_all(outgoing_back, 'det', split_axis=0, concat_axis=0, tiled=T...  190 us
    dot_general x4, matrix products, warp_group(): jnp.einsum('nik,nlk->nil', inner, right, preferred_element_type=jnp.float32)  45 us
    gather x4, local copies, waits for them, and re-layouts, warp_group(): left = jnp.take(warps, group_rows, axis=0)  19.9 us
    gather x4, local copies, waits for them, and re-layouts, warp_group(): right = jnp.take(warps, group_cols, axis=0)  19.7 us
    unnamed x18, local copies, waits for them, and re-layouts  17.5 us
    select_n x1, other arithmetic, shards(): outgoing = jnp.take(candidates, jnp.maximum(wanted, 0), axis=0)  14.1 us
    mul x1, other arithmetic, shards(): warp_tiles(outgoing, wanted_rows, wanted_cols, warps) * live[:, None, None]  14 us
  transfers between devices with their start and end apart: 5, of which 4 were waited for; matrix products, arithmetic and copies ran while one was open for 5% of the time, Pallas kernels for 0%

commit v1 on v0

v1 whole, which is shorter than its diff:
```python
import functools

import jax
import jax.numpy as jnp
from jax import lax
from jax.experimental import pallas as pl
from jax.experimental.pallas import tpu as pltpu
from jax.sharding import PartitionSpec as P

SIDE = 512
RING = 4
TILES = 2
PER_TILE = 4
BASES = 5
ROUND = (0, 1, 3, 2)
VMEM_LIMIT = 56 * 1024 * 1024


def place(z, y):
    return (z % RING) * RING + y % RING


def hop(block, dz, dy):
    route = [
        (place(z, y), place(z + dz, y + dy)) for z in range(RING) for y in range(RING)
    ]
    return lax.ppermute(block, "det", route)


def along(block, axis, step):
    return hop(block, step, 0) if axis == "z" else hop(block, 0, step)


def next_patch(block):
    count = lax.axis_size("sky")
    return lax.ppermute(block, "sky", [((i + 1) % count, i) for i in range(count)])


def spread_small(block, axis):
    return jnp.stack([block] + [along(block, axis, -k) for k in range(1, RING)])


def make_bands(taps):
    width = taps.shape[1]
    offsets = jnp.arange(SIDE)[None, :] - jnp.arange(SIDE)[:, None] + width // 2
    selector = (jnp.arange(width)[:, None, None] == offsets[None]).astype(jnp.float32)
    bands = jnp.einsum("tij,ft->fij", selector, taps, precision=lax.Precision.HIGHEST)
    return bands.astype(jnp.bfloat16)


def warp_kernel(steps, where, meta, *refs):
    cands, (warps, out), scratch = refs[:10], refs[10:12], refs[12:]
    picks, tile, left, right, acc, sems = scratch
    z, y = where[0], where[1]
    count = jnp.int32(0)
    for n, step in enumerate(steps):
        for t in range(TILES):
            for k in range(PER_TILE):
                q = meta[step, 0, t * PER_TILE + k]
                owner = (q // TILES) % (RING * RING)
                picks[0, count] = (
                    q // (TILES * RING * RING) * (RING * TILES)
                    + ((owner // RING - z + RING) % RING) * TILES
                    + q % TILES
                )
                picks[1, count] = meta[step, 1, t * PER_TILE + k]
                picks[2, count] = meta[step, 2, t * PER_TILE + k]
                picks[3, count] = n * TILES + t
                count = count + (owner % RING == y).astype(jnp.int32)

    def tile_copy(slot, source):
        return pltpu.make_async_copy(source, tile.at[slot], sems.at[0, slot])

    def bank_copies(slot, row, col):
        return (
            pltpu.make_async_copy(warps.at[row], left.at[slot], sems.at[1, slot]),
            pltpu.make_async_copy(warps.at[col], right.at[slot], sems.at[2, slot]),
        )

    def start(i, slot):
        source = picks[0, i]
        for copy in bank_copies(slot, picks[1, i], picks[2, i]):
            copy.start()
        for which in range(2):
            for dz in range(RING):
                for local in range(TILES):

                    @pl.when(source == (which * RING + dz) * TILES + local)
                    def _():
                        if dz == 2:
                            ref = cands[which * 5 + 3 + local].at[0]
                        else:
                            ref = cands[which * 5 + {0: 0, 3: 1, 1: 2}[dz]].at[local]
                        tile_copy(slot, ref).start()

    @pl.when(count > 0)
    def _():
        start(0, 0)

    acc[...] = jnp.zeros_like(acc)

    def body(i, carry):
        slot = lax.rem(i, 2)
        tile_copy(slot, cands[0].at[0]).wait()
        for copy in bank_copies(slot, 0, 0):
            copy.wait()

        @pl.when(i + 1 < count)
        def _():
            start(i + 1, 1 - slot)

        inner = jnp.dot(left[slot], tile[slot], preferred_element_type=jnp.float32)
        piece = lax.dot_general(
            inner.astype(jnp.bfloat16),
            right[slot],
            (((1,), (1,)), ((), ())),
            preferred_element_type=jnp.float32,
        )
        target = picks[3, i]
        acc[target] = acc[target] + piece
        return carry

    lax.fori_loop(0, count, body, 0)
    out[...] = acc[...].astype(jnp.bfloat16)


def warp_partials(steps, where, meta, cands, warps):
    rows = len(steps) * TILES
    anywhere = pl.BlockSpec(memory_space=pl.ANY)
    scalars = pl.BlockSpec(memory_space=pltpu.SMEM)
    return pl.pallas_call(
        functools.partial(warp_kernel, steps),
        out_shape=jax.ShapeDtypeStruct((rows, SIDE, SIDE), jnp.bfloat16),
        in_specs=[scalars, scalars] + [anywhere] * 11,
        out_specs=pl.BlockSpec(memory_space=pltpu.VMEM),
        scratch_shapes=[
            pltpu.SMEM((4, rows * PER_TILE + 1), jnp.int32),
            pltpu.VMEM((2, SIDE, SIDE), jnp.bfloat16),
            pltpu.VMEM((2, SIDE, SIDE), jnp.bfloat16),
            pltpu.VMEM((2, SIDE, SIDE), jnp.bfloat16),
            pltpu.VMEM((rows, SIDE, SIDE), jnp.float32),
            pltpu.SemaphoreType.DMA((3, 2)),
        ],
        compiler_params=pltpu.CompilerParams(vmem_limit_bytes=VMEM_LIMIT),
        cost_estimate=pl.CostEstimate(
            flops=rows * 4 * SIDE**3, bytes_accessed=rows * 4 * SIDE**2 * 2, transcendentals=0
        ),
    )(where, meta, *cands, warps)


def match_kernel(picks, coef, row, col, first, second, third, science, out, warped, model):
    b = pl.program_id(0)

    @pl.when(b == 0)
    def _():
        total = first[...].astype(jnp.float32) + second[...].astype(jnp.float32)
        warped[...] = (total + third[...].astype(jnp.float32)).astype(jnp.bfloat16)
        model[...] = jnp.zeros_like(model)

    half = jnp.dot(row[...], warped[...], preferred_element_type=jnp.float32)
    conv = lax.dot_general(
        half.astype(jnp.bfloat16),
        col[...],
        (((1,), (1,)), ((), ())),
        preferred_element_type=jnp.float32,
    )
    shape = (SIDE, SIDE)
    ui = (2.0 * lax.broadcasted_iota(jnp.int32, shape, 0).astype(jnp.float32) + 1.0) / SIDE - 1.0
    uj = (2.0 * lax.broadcasted_iota(jnp.int32, shape, 1).astype(jnp.float32) + 1.0) / SIDE - 1.0
    model[...] += (coef[b, 0] + coef[b, 1] * ui + coef[b, 2] * uj) * conv

    @pl.when(b == pl.num_programs(0) - 1)
    def _():
        out[...] = (science[...].astype(jnp.float32) - model[...]).astype(jnp.bfloat16)


def match(rows, cols, coef, bands, parts, science):
    whole = pl.BlockSpec((SIDE, SIDE), lambda b, picks: (0, 0))
    return pl.pallas_call(
        match_kernel,
        out_shape=jax.ShapeDtypeStruct((SIDE, SIDE), jnp.bfloat16),
        grid_spec=pltpu.PrefetchScalarGridSpec(
            num_scalar_prefetch=1,
            grid=(BASES,),
            in_specs=[
                pl.BlockSpec(memory_space=pltpu.SMEM),
                pl.BlockSpec((None, SIDE, SIDE), lambda b, picks: (picks[0, b], 0, 0)),
                pl.BlockSpec((None, SIDE, SIDE), lambda b, picks: (picks[1, b], 0, 0)),
                whole,
                whole,
                whole,
                whole,
            ],
            out_specs=whole,
            scratch_shapes=[
                pltpu.VMEM((SIDE, SIDE), jnp.bfloat16),
                pltpu.VMEM((SIDE, SIDE), jnp.float32),
            ],
        ),
        compiler_params=pltpu.CompilerParams(vmem_limit_bytes=VMEM_LIMIT),
        cost_estimate=pl.CostEstimate(
            flops=BASES * 4 * SIDE**3, bytes_accessed=BASES * 4 * SIDE**2 * 2, transcendentals=0
        ),
    )(jnp.stack([rows, cols]), coef, bands, bands, *parts, science)


def ring_gather(items, axis):
    other = {"z": 0, "y": 1}[axis]

    def moved(part, step, array, rows=None):
        away = list(part[1])
        away[other] -= step
        return (rows or part[0], tuple(away), array)

    found = list(items)
    if len(items) == 1:
        (part,) = items
        (low, high) = part[0]
        mid = (low + high) // 2
        ahead = moved(part, 1, along(part[2], axis, 1))
        back = moved(part, -1, along(part[2], axis, -1))
        found += [ahead, back]
        found.append(moved(ahead, 1, along(ahead[2][: mid - low], axis, 1), (low, mid)))
        found.append(moved(back, -1, along(back[2][mid - low :], axis, -1), (mid, high)))
        return found
    first = []
    for part in items:
        for step in (1, -1):
            first.append(moved(part, step, along(part[2], axis, step)))
    for n, step in enumerate((1, -1, 1, -1, -1)):
        part = first[2 * n + (0 if step == 1 else 1)]
        first.append(moved(part, step, along(part[2], axis, step)))
    return found + first


def return_kernel(plan, where, homes, *refs):
    arrays, out, sems = refs[: len(plan)], refs[-2], refs[-1]
    z, y = where[0], where[1]
    me = z * RING + y
    copies = []
    for n, (t, (low, high), (dz, dy)) in enumerate(plan):
        home = homes[dz % RING, dy % RING, t]
        source = ((z + dz + RING) % RING) * RING + (y + dy + RING) % RING
        slot = source * TILES + home % TILES
        copy = pltpu.make_async_copy(
            arrays[n], out.at[slot, pl.ds(low, high - low)], sems.at[n]
        )
        copies.append((home // TILES == me, copy))
    for live, copy in copies:
        pl.when(live)(copy.start)
    for live, copy in copies:
        pl.when(live)(copy.wait)


def give_back(where, homes, parts, blank):
    plan = [(t, rows, away) for t, found in enumerate(parts) for rows, away, _ in found]
    arrays = [array for found in parts for _, _, array in found]
    anywhere = pl.BlockSpec(memory_space=pl.ANY)
    scalars = pl.BlockSpec(memory_space=pltpu.SMEM)
    return pl.pallas_call(
        functools.partial(return_kernel, plan),
        out_shape=jax.ShapeDtypeStruct(blank.shape, blank.dtype),
        in_specs=[scalars, scalars] + [anywhere] * (len(plan) + 1),
        out_specs=anywhere,
        scratch_shapes=[pltpu.SemaphoreType.DMA((len(plan),))],
        input_output_aliases={len(plan) + 2: 0},
        compiler_params=pltpu.CompilerParams(vmem_limit_bytes=VMEM_LIMIT),
    )(where, homes, *arrays, blank)


def shards(
    templates,
    science,
    intersection,
    row_warp,
    col_warp,
    warps,
    taps,
    basis_row,
    basis_col,
    coef,
    home,
):
    me = lax.axis_index("det")
    where = jnp.stack([me // RING, me % RING]).astype(jnp.int32)

    with jax.named_scope("gather_templates"):
        before = along(templates, "z", 1)
        after = along(templates, "z", -1)
        far = (along(before[:1], "z", 1), along(after[1:], "z", -1))
        own = (templates, before, after) + far
        cands = own + tuple(next_patch(block) for block in own)

    with jax.named_scope("spread_tables"):
        table = jnp.concatenate(
            [
                intersection.reshape(-1),
                row_warp.reshape(-1),
                col_warp.reshape(-1),
                jnp.pad(home, (0, TILES * PER_TILE - TILES)),
            ]
        ).reshape(4, TILES * PER_TILE)
        meta = spread_small(table, "y")
        homes = spread_small(meta[:, 3, :TILES], "z")

    bands = make_bands(taps)
    blank = jnp.zeros((RING * RING * TILES, SIDE, SIDE), jnp.bfloat16)

    with jax.named_scope("warp"):
        opposite = warp_partials((2,), where, meta, cands, warps)
        nearer = warp_partials((0, 1, 3), where, meta, cands, warps)

    with jax.named_scope("sum_partials"):
        up = along(opposite[0], "y", 1)
        down = along(opposite[1], "y", -1)

        def plus(a, b):
            return (a.astype(jnp.float32) + b.astype(jnp.float32)).astype(jnp.bfloat16)

        parts = (
            (nearer[0], along(plus(nearer[2], up), "y", 1), along(nearer[4], "y", -1)),
            (nearer[1], along(nearer[3], "y", 1), along(plus(nearer[5], down), "y", -1)),
        )

    with jax.named_scope("match"):
        diffs = [
            match(basis_row[t], basis_col[t], coef[t], bands, parts[t], science[t])
            for t in range(TILES)
        ]

    with jax.named_scope("spread_differences"):
        whole = (0, SIDE)
        first = ring_gather(ring_gather([(whole, (0, 0), diffs[0])], "z"), "y")
        second = ring_gather(ring_gather([(whole, (0, 0), diffs[1])], "y"), "z")

    with jax.named_scope("give_back"):
        return give_back(where, homes, (first, second), blank)


def solution(mesh):
    placed = (
        P(("sky", "det"), None, None),
        P(("sky", "det"), None, None),
        P(("sky", "det"), None),
        P(("sky", "det"), None),
        P(("sky", "det"), None),
        P(),
        P(),
        P(("sky", "det"), None),
        P(("sky", "det"), None),
        P(("sky", "det"), None, None),
        P(("sky", "det")),
    )
    return jax.shard_map(
        shards, mesh=mesh, in_specs=placed, out_specs=P(("sky", "det"), None, None), check_vma=False
    )
```

time: 665 us -> 422 us (0.63)
  the two profiles are of different devices: /device:TPU:2 before, /device:TPU:120 now
where the time goes in v1:
time: 422 us; the launch traced here: 415 us
  Pallas kernels  163 us (39%)
  waiting for transfers between devices  122 us (29%)
  starting transfers between devices  75.5 us (18%)
  local copies, waits for them, and re-layouts  35.2 us (8%)
  matrix products  12.8 us (3%)
  other arithmetic  5.28 us (1%)
    pallas_call x1, Pallas kernels, give_back(): pl.pallas_call(functools.partial(return_kernel, plan), out_shape=jax.Shap...  129 us
    ppermute x54, waiting for transfers between devices, hop(): return lax.ppermute(block, 'det', route)  99.4 us
    ppermute x54, starting transfers between devices, hop(): return lax.ppermute(block, 'det', route)  71.4 us
    ppermute x5, waiting for transfers between devices, next_patch(): lax.ppermute(block, 'sky', [((i + 1) % count, i) for i in range(count)])  22.9 us
    pallas_call x2, Pallas kernels, warp_partials(): pl.pallas_call(functools.partial(warp_kernel, steps), out_shape=jax.Shape...  17.1 us
    pallas_call x2, Pallas kernels, match(): pl.pallas_call(match_kernel, out_shape=jax.ShapeDtypeStruct((SIDE, SIDE),...  16.5 us
    dot_general x1, matrix products, make_bands(): jnp.einsum('tij,ft->fij', selector, taps, precision=lax.Precision.HIGHEST)  12.8 us
    dot_general x1, local copies, waits for them, and re-layouts, make_bands(): jnp.einsum('tij,ft->fij', selector, taps, precision=lax.Precision.HIGHEST)  11.4 us
  transfers between devices with their start and end apart: 59, of which 22 were waited for; matrix products, arithmetic and copies ran while one was open for 10% of the time, Pallas kernels for 8%

profile of v1, /device:TPU:120, one launch (start us, length us, event | category | flops | bytes accessed | tf_op | source)
XLA Modules:
  0.0 414.9 jit_solution(16264731675662127718)
XLA Ops:
  0.4 2.8 collective-permute-start.6
  5.5 20.8 %collective-permute-done.7.refs_2_ = bf16[2,512,512]{2,1,0:T(8,128)(2,1)S(1)} collective-permute-done((bf16[2,512,512]{2,1,0:T(8,128)(2,1)}, bf16[2,512,512]{2,1,0:T(8,128)(2,1)S(1)}, u32[]{:S(2)}, u32[]{:S(2)}) %collective-permute-start.7) | collective-permute-done | bytes 1048608 | tf_op jit(solution)/shard_map/gather_templates/ppermute | solution.py:27
  28.1 3.2 collective-permute-start.8
  32.4 2.6 collective-permute-start.1
  41.1 2.3 slice_bitcast_fusion.8
  43.4 2.3 collective-permute-start.14
  45.7 12.8 %fusion = bf16[512,512,16]{1,2,0:T(8,128)(2,1)} fusion(s32[512,512]{1,0:T(8,128)S(1)} %subtract_add_fusion, f32[16,21]{1,0:T(8,128)S(1)} %copy-done), kind=kOutput, calls=%fused_computation.1 | convolution fusion | flops 1062469632 | bytes 9438528 | tf_op jit(solution)/shard_map/tij,ft->fij/dot_general | solution.py:47
  59.1 17.3 %collective-permute-done.14.refs_9_ = bf16[1,512,512]{2,1,0:T(8,128)(2,1)S(1)} collective-permute-done((bf16[1,512,512]{2,1,0:T(8,128)(2,1)S(1)}, bf16[1,512,512]{2,1,0:T(8,128)(2,1)S(1)}, u32[]{:S(2)}, u32[]{:S(2)}) %collective-permute-start.14) | collective-permute-done | bytes 524320 | tf_op jit(solution)/shard_map/gather_templates/ppermute | solution.py:36
  76.4 5.6 %collective-permute-done.13.refs_8_ = bf16[1,512,512]{2,1,0:T(8,128)(2,1)S(1)} collective-permute-done((bf16[1,512,512]{2,1,0:T(8,128)(2,1)S(1)}, bf16[1,512,512]{2,1,0:T(8,128)(2,1)S(1)}, u32[]{:S(2)}, u32[]{:S(2)}) %collective-permute-start.13) | collective-permute-done | bytes 524320 | tf_op jit(solution)/shard_map/gather_templates/ppermute | solution.py:36
  83.9 2.2 warp.3
  87.4 2.9 collective-permute-start.38
  90.2 3.3 collective-permute-start.15
  93.5 15.0 %warp.2 = bf16[6,512,512]{2,1,0:T(8,128)(2,1)} custom-call(s32[2]{0:T(128)} %pad_add_fusion.5.where, s32[4,4,8]{2,1,0:T(4,128)} %pad_add_fusion.meta, bf16[2,512,512]{2,1,0:T(8,128)(2,1)} %refs_0_.3, bf16[2,512,512]{2,1,0:T(8,128)(2,1)} %copy-done.3, bf16[2,512,512]{2,1,0:T(8,128)(2,1)} %copy-done.2, bf16[1,512,512]{2,1,0:T(8,128)(2,1)} %copy-done.9, ...), custom_call_target="tpu_custom_call" | custom-call | flops 3221225472 | bytes 12582912 | tf_op jit(solution)/shard_map/warp/pallas_call | solution.py:131
  108.5 2.9 slice_bitcast_fusion.2
  111.4 4.2 %collective-permute-start.17 = (bf16[512,512]{1,0:T(8,128)(2,1)}, bf16[512,512]{1,0:T(8,128)(2,1)S(1)}, u32[]{:S(2)}, u32[]{:S(2)}) collective-permute-start(bf16[512,512]{1,0:T(8,128)(2,1)} %get-tuple-element.9), channel_id=1, source_target_pairs={{0,3},{1,0},{2,1},{3,2},{4,7},{5,4},{6,5},{7,6},{8,11},{9,8},{10,9... | collective-permute-start | bytes 1572872 | tf_op jit(solution)/shard_map/sum_partials/ppermute | solution.py:27
  117.2 2.2 collective-permute-start.39
  120.1 11.4 %copy.37 = bf16[512,512,16]{1,0,2:T(8,128)(2,1)} copy(bf16[512,512,16]{1,2,0:T(8,128)(2,1)} %fusion) | data formatting | bytes 16777216 | tf_op jit(solution)/shard_map/tij,ft->fij/dot_general | solution.py:47
  133.1 8.0 %match.2.refs_0_ = bf16[512,512]{1,0:T(8,128)(2,1)} custom-call(s32[2,5]{1,0:T(2,128)} %pad_add_fusion.2.picks, f32[5,3]{1,0:T(8,128)} %bitcast.49, bf16[16,512,512]{2,1,0:T(8,128)(2,1)} %bitcast.44, bf16[16,512,512]{2,1,0:T(8,128)(2,1)} %bitcast.45, bf16[512,512]{1,0:T(8,128)(2,1)} %get-tuple-element.10.first, bf16[512,512]{1,0:T(8,128)(2,1)} %copy-done.26, ...), custom_call_target="tpu_custom_call" | custom-call | flops 2684354560 | bytes 10485760 | tf_op jit(solution)/shard_map/match/pallas_call | solution.py:179
  141.1 3.2 collective-permute-start.18
  146.6 8.5 %match.3.refs_20_ = bf16[512,512]{1,0:T(8,128)(2,1)} custom-call(s32[2,5]{1,0:T(2,128)} %pad_add_fusion.3.picks, f32[5,3]{1,0:T(8,128)} %bitcast.50, bf16[16,512,512]{2,1,0:T(8,128)(2,1)} %bitcast.46, bf16[16,512,512]{2,1,0:T(8,128)(2,1)} %bitcast.47, bf16[512,512]{1,0:T(8,128)(2,1)} %get-tuple-element.8.first, bf16[512,512]{1,0:T(8,128)(2,1)} %copy-done.23, ...), custom_call_target="tpu_custom_call" | custom-call | flops 2684354560 | bytes 10485760 | tf_op jit(solution)/shard_map/match/pallas_call | solution.py:179
  155.0 1.9 collective-permute-start.41
  159.0 2.5 collective-permute-start.22
  161.5 9.8 %collective-permute-done.41.refs_22_ = bf16[512,512]{1,0:T(8,128)(2,1)S(1)} collective-permute-done((bf16[512,512]{1,0:T(8,128)(2,1)}, bf16[512,512]{1,0:T(8,128)(2,1)S(1)}, u32[]{:S(2)}, u32[]{:S(2)}) %collective-permute-start.41) | collective-permute-done | bytes 524320 | tf_op jit(solution)/shard_map/spread_differences/ppermute | solution.py:27
  173.2 7.7 %collective-permute-done.5 = s32[4,2]{0,1:T(2,128)S(1)} collective-permute-done((s32[4,2]{0,1:T(2,128)S(1)}, s32[4,2]{0,1:T(2,128)S(1)}, u32[]{:S(2)}, u32[]{:S(2)}) %collective-permute-start.5) | collective-permute-done | bytes 64 | tf_op jit(solution)/shard_map/spread_tables/ppermute | solution.py:27
  181.1 4.8 %collective-permute-done.4 = s32[4,2]{0,1:T(2,128)S(1)} collective-permute-done((s32[4,2]{0,1:T(2,128)S(1)}, s32[4,2]{0,1:T(2,128)S(1)}, u32[]{:S(2)}, u32[]{:S(2)}) %collective-permute-start.4) | collective-permute-done | bytes 64 | tf_op jit(solution)/shard_map/spread_tables/ppermute | solution.py:27
  186.2 4.5 %collective-permute-done.3 = s32[4,2]{0,1:T(2,128)S(1)} collective-permute-done((s32[4,2]{0,1:T(2,128)S(1)}, s32[4,2]{0,1:T(2,128)S(1)}, u32[]{:S(2)}, u32[]{:S(2)}) %collective-permute-start.3) | collective-permute-done | bytes 64 | tf_op jit(solution)/shard_map/spread_tables/ppermute | solution.py:27
  190.7 3.2 collective-permute-start.20
  194.2 3.0 collective-permute-start.42
  199.2 2.3 collective-permute-start.26
  201.5 2.9 collective-permute-done.43.refs_24_
  204.4 3.2 collective-permute-start.24
  207.7 7.6 %collective-permute-done.32.refs_15_ = bf16[512,512]{1,0:T(8,128)(2,1)S(1)} collective-permute-done((bf16[512,512]{1,0:T(8,128)(2,1)}, bf16[512,512]{1,0:T(8,128)(2,1)S(1)}, u32[]{:S(2)}, u32[]{:S(2)}) %collective-permute-start.32) | collective-permute-done | bytes 524320 | tf_op jit(solution)/shard_map/spread_differences/ppermute | solution.py:27
  215.6 1.7 collective-permute-start.49
  217.3 4.7 %collective-permute-done.26.refs_9_ = bf16[512,512]{1,0:T(8,128)(2,1)} collective-permute-done((bf16[512,512]{1,0:T(8,128)(2,1)S(1)}, bf16[512,512]{1,0:T(8,128)(2,1)}, u32[]{:S(2)}, u32[]{:S(2)}) %collective-permute-start.26) | collective-permute-done | bytes 524320 | tf_op jit(solution)/shard_map/spread_differences/ppermute | solution.py:27
  222.1 2.0 collective-permute-start.47
  224.1 8.2 %collective-permute-done.24.refs_7_ = bf16[512,512]{1,0:T(8,128)(2,1)S(1)} collective-permute-done((bf16[512,512]{1,0:T(8,128)(2,1)S(1)}, bf16[512,512]{1,0:T(8,128)(2,1)S(1)}, u32[]{:S(2)}, u32[]{:S(2)}) %collective-permute-start.24) | collective-permute-done | bytes 524320 | tf_op jit(solution)/shard_map/spread_differences/ppermute | solution.py:27
  232.4 3.8 collective-permute-start.30
  236.9 3.4 collective-permute-start.28
  240.3 6.9 %collective-permute-done.46.refs_27_ = bf16[512,512]{1,0:T(8,128)(2,1)S(1)} collective-permute-done((bf16[512,512]{1,0:T(8,128)(2,1)S(1)}, bf16[512,512]{1,0:T(8,128)(2,1)S(1)}, u32[]{:S(2)}, u32[]{:S(2)}) %collective-permute-start.46) | collective-permute-done | bytes 524320 | tf_op jit(solution)/shard_map/spread_differences/ppermute | solution.py:27
  247.2 3.3 collective-permute-start.52
  250.6 3.3 collective-permute-start.50
  254.0 2.2 collective-permute-done.53.refs_34_
  257.3 3.6 collective-permute-start.34
  262.0 3.6 collective-permute-start.56
  265.7 3.7 collective-permute-done.58.refs_39_
  271.0 8.2 %collective-permute-done.57.refs_38_ = bf16[256,512]{1,0:T(8,128)(2,1)} collective-permute-done((bf16[256,512]{1,0:T(8,128)(2,1)}, bf16[256,512]{1,0:T(8,128)(2,1)}, u32[]{:S(2)}, u32[]{:S(2)}) %collective-permute-start.57) | collective-permute-done | bytes 262176 | tf_op jit(solution)/shard_map/spread_differences/ppermute | solution.py:27
  279.2 6.0 %broadcast_in_dim.2.refs_40_ = bf16[32,512,512]{2,1,0:T(8,128)(2,1)} broadcast(bf16[]{:T(256)} %constant.34.clone.1), dimensions={} | broadcast | bytes 16777218 | tf_op jit(solution)/shard_map/broadcast_in_dim | solution.py:307
  285.3 129.4 %give_back.1 = bf16[32,512,512]{2,1,0:T(8,128)(2,1)} custom-call(s32[2]{0:T(128)} %pad_add_fusion.5.where, s32[4,4,2]{2,1,0:T(4,128)} %pad_add_fusion.1.homes, bf16[512,512]{1,0:T(8,128)(2,1)} %match.2.refs_0_, bf16[512,512]{1,0:T(8,128)(2,1)} %copy-done.13, bf16[512,512]{1,0:T(8,128)(2,1)} %copy-done.12, ...), custom_call_target="tpu_custom_call", output_to_operand_aliasing={{}: (42, {})} | custom-call | tf_op jit(solution)/shard_map/give_back/pallas_call | solution.py:260
  (197 shorter events, 33.4 us)
Async XLA Ops:
  0.0 26.3 %collective-permute-start.7 = (bf16[2,512,512]{2,1,0:T(8,128)(2,1)}, bf16[2,512,512]{2,1,0:T(8,128)(2,1)S(1)}, u32[]{:S(2)}, u32[]{:S(2)}) collective-permute-start(bf16[2,512,512]{2,1,0:T(8,128)(2,1)} %refs_0_.3), channel_id=1, source_target_pairs={{0,12},{1,13},{2,14},{3,15},{4,0},{5,1},{6,2},{7,3},{8,4},{9,5},{1... | collective-permute-start | bytes 3145736 | tf_op jit(solution)/shard_map/gather_templates/ppermute | solution.py:27
  0.4 26.8 %collective-permute-start.6 = (bf16[2,512,512]{2,1,0:T(8,128)(2,1)}, bf16[2,512,512]{2,1,0:T(8,128)(2,1)S(1)}, u32[]{:S(2)}, u32[]{:S(2)}) collective-permute-start(bf16[2,512,512]{2,1,0:T(8,128)(2,1)} %refs_0_.3), channel_id=1, source_target_pairs={{0,4},{1,5},{2,6},{3,7},{4,8},{5,9},{6,10},{7,11},{8,12},{9,13},{1... | collective-permute-start | bytes 3145736 | tf_op jit(solution)/shard_map/gather_templates/ppermute | solution.py:27
  27.2 16.2 %collective-permute-start.9 = (bf16[1,512,512]{2,1,0:T(8,128)(2,1)}, bf16[1,512,512]{2,1,0:T(8,128)(2,1)S(1)}, u32[]{:S(2)}, u32[]{:S(2)}) collective-permute-start(bf16[1,512,512]{2,1,0:T(8,128)(2,1)} %slice.94), channel_id=1, source_target_pairs={{0,12},{1,13},{2,14},{3,15},{4,0},{5,1},{6,2},{7,3},{8,4},{9,5},{1... | collective-permute-start | bytes 1572872 | tf_op jit(solution)/shard_map/gather_templates/ppermute | solution.py:27
  28.1 17.6 %collective-permute-start.8 = (bf16[1,512,512]{2,1,0:T(8,128)(2,1)}, bf16[1,512,512]{2,1,0:T(8,128)(2,1)S(1)}, u32[]{:S(2)}, u32[]{:S(2)}) collective-permute-start(bf16[1,512,512]{2,1,0:T(8,128)(2,1)} %slice.93), channel_id=1, source_target_pairs={{0,4},{1,5},{2,6},{3,7},{4,8},{5,9},{6,10},{7,11},{8,12},{9,13},{1... | collective-permute-start | bytes 1572872 | tf_op jit(solution)/shard_map/gather_templates/ppermute | solution.py:27
  35.8 23.4 %collective-permute-start.10 = (bf16[2,512,512]{2,1,0:T(8,128)(2,1)}, bf16[2,512,512]{2,1,0:T(8,128)(2,1)S(1)}, u32[]{:S(2)}, u32[]{:S(2)}) collective-permute-start(bf16[2,512,512]{2,1,0:T(8,128)(2,1)} %refs_0_.3), channel_id=1, source_target_pairs={{16,0},{32,16},{48,32},{64,48},{80,64},{96,80},{112,96},{0,112},{1... | collective-permute-start | bytes 3145736 | tf_op jit(solution)/shard_map/gather_templates/ppermute | solution.py:36
  37.5 38.9 %collective-permute-start.12 = (bf16[2,512,512]{2,1,0:T(8,128)(2,1)S(1)}, bf16[2,512,512]{2,1,0:T(8,128)(2,1)S(1)}, u32[]{:S(2)}, u32[]{:S(2)}) collective-permute-start(bf16[2,512,512]{2,1,0:T(8,128)(2,1)S(1)} %collective-permute-done.7.refs_2_), channel_id=1, source_target_pairs={{16,0},{32,16},{48,32},{64,48},{80,64},{96,80},{112,96},{0,112},{1... | collective-permute-start | bytes 3145736 | tf_op jit(solution)/shard_map/gather_templates/ppermute | solution.py:36
  39.8 43.0 %collective-permute-start.11 = (bf16[2,512,512]{2,1,0:T(8,128)(2,1)S(1)}, bf16[2,512,512]{2,1,0:T(8,128)(2,1)S(1)}, u32[]{:S(2)}, u32[]{:S(2)}) collective-permute-start(bf16[2,512,512]{2,1,0:T(8,128)(2,1)S(1)} %collective-permute-done.6.refs_1_), channel_id=1, source_target_pairs={{16,0},{32,16},{48,32},{64,48},{80,64},{96,80},{112,96},{0,112},{1... | collective-permute-start | bytes 3145736 | tf_op jit(solution)/shard_map/gather_templates/ppermute | solution.py:36
  43.4 33.0 %collective-permute-start.14 = (bf16[1,512,512]{2,1,0:T(8,128)(2,1)S(1)}, bf16[1,512,512]{2,1,0:T(8,128)(2,1)S(1)}, u32[]{:S(2)}, u32[]{:S(2)}) collective-permute-start(bf16[1,512,512]{2,1,0:T(8,128)(2,1)S(1)} %collective-permute-done.9.refs_4_), channel_id=1, source_target_pairs={{16,0},{32,16},{48,32},{64,48},{80,64},{96,80},{112,96},{0,112},{1... | collective-permute-start | bytes 1572872 | tf_op jit(solution)/shard_map/gather_templates/ppermute | solution.py:36
  45.7 36.3 %collective-permute-start.13 = (bf16[1,512,512]{2,1,0:T(8,128)(2,1)S(1)}, bf16[1,512,512]{2,1,0:T(8,128)(2,1)S(1)}, u32[]{:S(2)}, u32[]{:S(2)}) collective-permute-start(bf16[1,512,512]{2,1,0:T(8,128)(2,1)S(1)} %collective-permute-done.8.refs_3_), channel_id=1, source_target_pairs={{16,0},{32,16},{48,32},{64,48},{80,64},{96,80},{112,96},{0,112},{1... | collective-permute-start | bytes 1572872 | tf_op jit(solution)/shard_map/gather_templates/ppermute | solution.py:36
  87.4 28.2 %collective-permute-start.38 = (bf16[512,512]{1,0:T(8,128)(2,1)S(1)}, bf16[512,512]{1,0:T(8,128)(2,1)S(1)}, u32[]{:S(2)}, u32[]{:S(2)}) collective-permute-start(bf16[512,512]{1,0:T(8,128)(2,1)S(1)} %get-tuple-element.13), channel_id=1, source_target_pairs={{0,3},{1,0},{2,1},{3,2},{4,7},{5,4},{6,5},{7,6},{8,11},{9,8},{10,9... | collective-permute-start | bytes 1572872 | tf_op jit(solution)/shard_map/sum_partials/ppermute | solution.py:27
  90.2 25.3 %collective-permute-start.15 = (bf16[512,512]{1,0:T(8,128)(2,1)S(1)}, bf16[512,512]{1,0:T(8,128)(2,1)S(1)}, u32[]{:S(2)}, u32[]{:S(2)}) collective-permute-start(bf16[512,512]{1,0:T(8,128)(2,1)S(1)} %get-tuple-element.14), channel_id=1, source_target_pairs={{0,1},{1,2},{2,3},{3,0},{4,5},{5,6},{6,7},{7,4},{8,9},{9,10},{10,1... | collective-permute-start | bytes 1572872 | tf_op jit(solution)/shard_map/sum_partials/ppermute | solution.py:27
  111.4 20.8 %collective-permute-start.17 = (bf16[512,512]{1,0:T(8,128)(2,1)}, bf16[512,512]{1,0:T(8,128)(2,1)S(1)}, u32[]{:S(2)}, u32[]{:S(2)}) collective-permute-start(bf16[512,512]{1,0:T(8,128)(2,1)} %get-tuple-element.9), channel_id=1, source_target_pairs={{0,3},{1,0},{2,1},{3,2},{4,7},{5,4},{6,5},{7,6},{8,11},{9,8},{10,9... | collective-permute-start | bytes 1572872 | tf_op jit(solution)/shard_map/sum_partials/ppermute | solution.py:27
  117.0 15.1 %collective-permute-start.16 = (bf16[512,512]{1,0:T(8,128)(2,1)S(1)}, bf16[512,512]{1,0:T(8,128)(2,1)S(1)}, u32[]{:S(2)}, u32[]{:S(2)}) collective-permute-start(bf16[512,512]{1,0:T(8,128)(2,1)S(1)} %get-tuple-element.6), channel_id=1, source_target_pairs={{0,1},{1,2},{2,3},{3,0},{4,5},{5,6},{6,7},{7,4},{8,9},{9,10},{10,1... | collective-permute-start | bytes 1572872 | tf_op jit(solution)/shard_map/sum_partials/ppermute | solution.py:27
  117.1 28.5 %collective-permute-start.37 = (bf16[512,512]{1,0:T(8,128)(2,1)}, bf16[512,512]{1,0:T(8,128)(2,1)S(1)}, u32[]{:S(2)}, u32[]{:S(2)}) collective-permute-start(bf16[512,512]{1,0:T(8,128)(2,1)} %get-tuple-element.7), channel_id=1, source_target_pairs={{0,1},{1,2},{2,3},{3,0},{4,5},{5,6},{6,7},{7,4},{8,9},{9,10},{10,1... | collective-permute-start | bytes 1572872 | tf_op jit(solution)/shard_map/sum_partials/ppermute | solution.py:27
  117.2 28.4 %collective-permute-start.39 = (bf16[512,512]{1,0:T(8,128)(2,1)S(1)}, bf16[512,512]{1,0:T(8,128)(2,1)S(1)}, u32[]{:S(2)}, u32[]{:S(2)}) collective-permute-start(bf16[512,512]{1,0:T(8,128)(2,1)S(1)} %get-tuple-element.5), channel_id=1, source_target_pairs={{0,3},{1,0},{2,1},{3,2},{4,7},{5,4},{6,5},{7,6},{8,11},{9,8},{10,9... | collective-permute-start | bytes 1572872 | tf_op jit(solution)/shard_map/sum_partials/ppermute | solution.py:27
  141.1 17.9 %collective-permute-start.19 = (bf16[512,512]{1,0:T(8,128)(2,1)}, bf16[512,512]{1,0:T(8,128)(2,1)S(1)}, u32[]{:S(2)}, u32[]{:S(2)}) collective-permute-start(bf16[512,512]{1,0:T(8,128)(2,1)} %match.2.refs_0_), channel_id=1, source_target_pairs={{0,12},{1,13},{2,14},{3,15},{4,0},{5,1},{6,2},{7,3},{8,4},{9,5},{1... | collective-permute-start | bytes 1572872 | tf_op jit(solution)/shard_map/spread_differences/ppermute | solution.py:27
  141.1 20.4 %collective-permute-start.18 = (bf16[512,512]{1,0:T(8,128)(2,1)}, bf16[512,512]{1,0:T(8,128)(2,1)S(1)}, u32[]{:S(2)}, u32[]{:S(2)}) collective-permute-start(bf16[512,512]{1,0:T(8,128)(2,1)} %match.2.refs_0_), channel_id=1, source_target_pairs={{0,4},{1,5},{2,6},{3,7},{4,8},{5,9},{6,10},{7,11},{8,12},{9,13},{1... | collective-permute-start | bytes 1572872 | tf_op jit(solution)/shard_map/spread_differences/ppermute | solution.py:27
  155.0 16.3 %collective-permute-start.41 = (bf16[512,512]{1,0:T(8,128)(2,1)}, bf16[512,512]{1,0:T(8,128)(2,1)S(1)}, u32[]{:S(2)}, u32[]{:S(2)}) collective-permute-start(bf16[512,512]{1,0:T(8,128)(2,1)} %match.3.refs_20_), channel_id=1, source_target_pairs={{0,3},{1,0},{2,1},{3,2},{4,7},{5,4},{6,5},{7,6},{8,11},{9,8},{10,9... | collective-permute-start | bytes 1572872 | tf_op jit(solution)/shard_map/spread_differences/ppermute | solution.py:27
  157.0 16.1 %collective-permute-start.40 = (bf16[512,512]{1,0:T(8,128)(2,1)}, bf16[512,512]{1,0:T(8,128)(2,1)S(1)}, u32[]{:S(2)}, u32[]{:S(2)}) collective-permute-start(bf16[512,512]{1,0:T(8,128)(2,1)} %match.3.refs_20_), channel_id=1, source_target_pairs={{0,1},{1,2},{2,3},{3,0},{4,5},{5,6},{6,7},{7,4},{8,9},{9,10},{10,1... | collective-permute-start | bytes 1572872 | tf_op jit(solution)/shard_map/spread_differences/ppermute | solution.py:27
  158.3 32.4 %collective-permute-start.23 = (bf16[512,512]{1,0:T(8,128)(2,1)S(1)}, bf16[512,512]{1,0:T(8,128)(2,1)S(1)}, u32[]{:S(2)}, u32[]{:S(2)}) collective-permute-start(bf16[512,512]{1,0:T(8,128)(2,1)S(1)} %copy-done.7), channel_id=1, source_target_pairs={{0,3},{1,0},{2,1},{3,2},{4,7},{5,4},{6,5},{7,6},{8,11},{9,8},{10,9... | collective-permute-start | bytes 1572872 | tf_op jit(solution)/shard_map/spread_differences/ppermute | solution.py:27
  159.0 34.9 %collective-permute-start.22 = (bf16[512,512]{1,0:T(8,128)(2,1)S(1)}, bf16[512,512]{1,0:T(8,128)(2,1)}, u32[]{:S(2)}, u32[]{:S(2)}) collective-permute-start(bf16[512,512]{1,0:T(8,128)(2,1)S(1)} %copy-done.7), channel_id=1, source_target_pairs={{0,1},{1,2},{2,3},{3,0},{4,5},{5,6},{6,7},{7,4},{8,9},{9,10},{10,1... | collective-permute-start | bytes 1572872 | tf_op jit(solution)/shard_map/spread_differences/ppermute | solution.py:27
  161.5 32.7 %collective-permute-start.45 = (bf16[512,512]{1,0:T(8,128)(2,1)}, bf16[512,512]{1,0:T(8,128)(2,1)}, u32[]{:S(2)}, u32[]{:S(2)}) collective-permute-start(bf16[512,512]{1,0:T(8,128)(2,1)} %match.3.refs_20_), channel_id=1, source_target_pairs={{0,12},{1,13},{2,14},{3,15},{4,0},{5,1},{6,2},{7,3},{8,4},{9,5},{1... | collective-permute-start | bytes 1572872 | tf_op jit(solution)/shard_map/spread_differences/ppermute | solution.py:27
  171.3 25.9 %collective-permute-start.44 = (bf16[512,512]{1,0:T(8,128)(2,1)}, bf16[512,512]{1,0:T(8,128)(2,1)}, u32[]{:S(2)}, u32[]{:S(2)}) collective-permute-start(bf16[512,512]{1,0:T(8,128)(2,1)} %match.3.refs_20_), channel_id=1, source_target_pairs={{0,4},{1,5},{2,6},{3,7},{4,8},{5,9},{6,10},{7,11},{8,12},{9,13},{1... | collective-permute-start | bytes 1572872 | tf_op jit(solution)/shard_map/spread_differences/ppermute | solution.py:27
  194.0 10.5 %collective-permute-start.43 = (bf16[256,512]{1,0:T(8,128)(2,1)S(1)}, bf16[256,512]{1,0:T(8,128)(2,1)S(1)}, u32[]{:S(2)}, u32[]{:S(2)}) collective-permute-start(bf16[256,512]{1,0:T(8,128)(2,1)S(1)} %slice.106), channel_id=1, source_target_pairs={{0,3},{1,0},{2,1},{3,2},{4,7},{5,4},{6,5},{7,6},{8,11},{9,8},{10,9... | collective-permute-start | bytes 786440 | tf_op jit(solution)/shard_map/spread_differences/ppermute | solution.py:27
  194.2 10.2 %collective-permute-start.42 = (bf16[256,512]{1,0:T(8,128)(2,1)S(1)}, bf16[256,512]{1,0:T(8,128)(2,1)S(1)}, u32[]{:S(2)}, u32[]{:S(2)}) collective-permute-start(bf16[256,512]{1,0:T(8,128)(2,1)S(1)} %slice.105), channel_id=1, source_target_pairs={{0,1},{1,2},{2,3},{3,0},{4,5},{5,6},{6,7},{7,4},{8,9},{9,10},{10,1... | collective-permute-start | bytes 786440 | tf_op jit(solution)/shard_map/spread_differences/ppermute | solution.py:27
  197.2 18.1 %collective-permute-start.32 = (bf16[512,512]{1,0:T(8,128)(2,1)}, bf16[512,512]{1,0:T(8,128)(2,1)S(1)}, u32[]{:S(2)}, u32[]{:S(2)}) collective-permute-start(bf16[512,512]{1,0:T(8,128)(2,1)} %collective-permute-done.22.refs_5_), channel_id=1, source_target_pairs={{0,1},{1,2},{2,3},{3,0},{4,5},{5,6},{6,7},{7,4},{8,9},{9,10},{10,1... | collective-permute-start | bytes 1572872 | tf_op jit(solution)/shard_map/spread_differences/ppermute | solution.py:27
  198.3 17.3 %collective-permute-start.27 = (bf16[512,512]{1,0:T(8,128)(2,1)S(1)}, bf16[512,512]{1,0:T(8,128)(2,1)S(1)}, u32[]{:S(2)}, u32[]{:S(2)}) collective-permute-start(bf16[512,512]{1,0:T(8,128)(2,1)S(1)} %collective-permute-done.19.refs_2_), channel_id=1, source_target_pairs={{0,3},{1,0},{2,1},{3,2},{4,7},{5,4},{6,5},{7,6},{8,11},{9,8},{10,9... | collective-permute-start | bytes 1572872 | tf_op jit(solution)/shard_map/spread_differences/ppermute | solution.py:27
  199.2 22.8 %collective-permute-start.26 = (bf16[512,512]{1,0:T(8,128)(2,1)S(1)}, bf16[512,512]{1,0:T(8,128)(2,1)}, u32[]{:S(2)}, u32[]{:S(2)}) collective-permute-start(bf16[512,512]{1,0:T(8,128)(2,1)S(1)} %collective-permute-done.19.refs_2_), channel_id=1, source_target_pairs={{0,1},{1,2},{2,3},{3,0},{4,5},{5,6},{6,7},{7,4},{8,9},{9,10},{10,1... | collective-permute-start | bytes 1572872 | tf_op jit(solution)/shard_map/spread_differences/ppermute | solution.py:27
  204.4 17.6 %collective-permute-start.25 = (bf16[512,512]{1,0:T(8,128)(2,1)S(1)}, bf16[512,512]{1,0:T(8,128)(2,1)}, u32[]{:S(2)}, u32[]{:S(2)}) collective-permute-start(bf16[512,512]{1,0:T(8,128)(2,1)S(1)} %collective-permute-done.18.refs_1_), channel_id=1, source_target_pairs={{0,3},{1,0},{2,1},{3,2},{4,7},{5,4},{6,5},{7,6},{8,11},{9,8},{10,9... | collective-permute-start | bytes 1572872 | tf_op jit(solution)/shard_map/spread_differences/ppermute | solution.py:27
  204.4 27.9 %collective-permute-start.24 = (bf16[512,512]{1,0:T(8,128)(2,1)S(1)}, bf16[512,512]{1,0:T(8,128)(2,1)S(1)}, u32[]{:S(2)}, u32[]{:S(2)}) collective-permute-start(bf16[512,512]{1,0:T(8,128)(2,1)S(1)} %collective-permute-done.18.refs_1_), channel_id=1, source_target_pairs={{0,1},{1,2},{2,3},{3,0},{4,5},{5,6},{6,7},{7,4},{8,9},{9,10},{10,1... | collective-permute-start | bytes 1572872 | tf_op jit(solution)/shard_map/spread_differences/ppermute | solution.py:27
  215.3 17.0 %collective-permute-start.54 = (bf16[512,512]{1,0:T(8,128)(2,1)}, bf16[512,512]{1,0:T(8,128)(2,1)S(1)}, u32[]{:S(2)}, u32[]{:S(2)}) collective-permute-start(bf16[512,512]{1,0:T(8,128)(2,1)} %collective-permute-done.44.refs_25_), channel_id=1, source_target_pairs={{0,4},{1,5},{2,6},{3,7},{4,8},{5,9},{6,10},{7,11},{8,12},{9,13},{1... | collective-permute-start | bytes 1572872 | tf_op jit(solution)/shard_map/spread_differences/ppermute | solution.py:27
  215.6 16.8 %collective-permute-start.49 = (bf16[512,512]{1,0:T(8,128)(2,1)S(1)}, bf16[512,512]{1,0:T(8,128)(2,1)S(1)}, u32[]{:S(2)}, u32[]{:S(2)}) collective-permute-start(bf16[512,512]{1,0:T(8,128)(2,1)S(1)} %collective-permute-done.41.refs_22_), channel_id=1, source_target_pairs={{0,12},{1,13},{2,14},{3,15},{4,0},{5,1},{6,2},{7,3},{8,4},{9,5},{1... | collective-permute-start | bytes 1572872 | tf_op jit(solution)/shard_map/spread_differences/ppermute | solution.py:27
  222.0 14.8 %collective-permute-start.48 = (bf16[512,512]{1,0:T(8,128)(2,1)S(1)}, bf16[512,512]{1,0:T(8,128)(2,1)}, u32[]{:S(2)}, u32[]{:S(2)}) collective-permute-start(bf16[512,512]{1,0:T(8,128)(2,1)S(1)} %collective-permute-done.41.refs_22_), channel_id=1, source_target_pairs={{0,4},{1,5},{2,6},{3,7},{4,8},{5,9},{6,10},{7,11},{8,12},{9,13},{1... | collective-permute-start | bytes 1572872 | tf_op jit(solution)/shard_map/spread_differences/ppermute | solution.py:27
  222.1 14.8 %collective-permute-start.47 = (bf16[512,512]{1,0:T(8,128)(2,1)S(1)}, bf16[512,512]{1,0:T(8,128)(2,1)}, u32[]{:S(2)}, u32[]{:S(2)}) collective-permute-start(bf16[512,512]{1,0:T(8,128)(2,1)S(1)} %collective-permute-done.40.refs_21_), channel_id=1, source_target_pairs={{0,12},{1,13},{2,14},{3,15},{4,0},{5,1},{6,2},{7,3},{8,4},{9,5},{1... | collective-permute-start | bytes 1572872 | tf_op jit(solution)/shard_map/spread_differences/ppermute | solution.py:27
  232.3 14.9 %collective-permute-start.46 = (bf16[512,512]{1,0:T(8,128)(2,1)S(1)}, bf16[512,512]{1,0:T(8,128)(2,1)S(1)}, u32[]{:S(2)}, u32[]{:S(2)}) collective-permute-start(bf16[512,512]{1,0:T(8,128)(2,1)S(1)} %collective-permute-done.40.refs_21_), channel_id=1, source_target_pairs={{0,4},{1,5},{2,6},{3,7},{4,8},{5,9},{6,10},{7,11},{8,12},{9,13},{1... | collective-permute-start | bytes 1572872 | tf_op jit(solution)/shard_map/spread_differences/ppermute | solution.py:27
  232.3 14.9 %collective-permute-start.31 = (bf16[256,512]{1,0:T(8,128)(2,1)S(1)}, bf16[256,512]{1,0:T(8,128)(2,1)S(1)}, u32[]{:S(2)}, u32[]{:S(2)}) collective-permute-start(bf16[256,512]{1,0:T(8,128)(2,1)S(1)} %collective-permute-done.21.refs_4_), channel_id=1, source_target_pairs={{0,3},{1,0},{2,1},{3,2},{4,7},{5,4},{6,5},{7,6},{8,11},{9,8},{10,9... | collective-permute-start | bytes 786440 | tf_op jit(solution)/shard_map/spread_differences/ppermute | solution.py:27
  232.4 18.1 %collective-permute-start.30 = (bf16[256,512]{1,0:T(8,128)(2,1)S(1)}, bf16[256,512]{1,0:T(8,128)(2,1)S(1)}, u32[]{:S(2)}, u32[]{:S(2)}) collective-permute-start(bf16[256,512]{1,0:T(8,128)(2,1)S(1)} %collective-permute-done.21.refs_4_), channel_id=1, source_target_pairs={{0,1},{1,2},{2,3},{3,0},{4,5},{5,6},{6,7},{7,4},{8,9},{9,10},{10,1... | collective-permute-start | bytes 786440 | tf_op jit(solution)/shard_map/spread_differences/ppermute | solution.py:27
  236.9 13.7 %collective-permute-start.29 = (bf16[256,512]{1,0:T(8,128)(2,1)S(1)}, bf16[256,512]{1,0:T(8,128)(2,1)S(1)}, u32[]{:S(2)}, u32[]{:S(2)}) collective-permute-start(bf16[256,512]{1,0:T(8,128)(2,1)S(1)} %collective-permute-done.20.refs_3_), channel_id=1, source_target_pairs={{0,3},{1,0},{2,1},{3,2},{4,7},{5,4},{6,5},{7,6},{8,11},{9,8},{10,9... | collective-permute-start | bytes 786440 | tf_op jit(solution)/shard_map/spread_differences/ppermute | solution.py:27
  236.9 17.0 %collective-permute-start.28 = (bf16[256,512]{1,0:T(8,128)(2,1)S(1)}, bf16[256,512]{1,0:T(8,128)(2,1)S(1)}, u32[]{:S(2)}, u32[]{:S(2)}) collective-permute-start(bf16[256,512]{1,0:T(8,128)(2,1)S(1)} %collective-permute-done.20.refs_3_), channel_id=1, source_target_pairs={{0,1},{1,2},{2,3},{3,0},{4,5},{5,6},{6,7},{7,4},{8,9},{9,10},{10,1... | collective-permute-start | bytes 786440 | tf_op jit(solution)/shard_map/spread_differences/ppermute | solution.py:27
  247.2 10.0 %collective-permute-start.52 = (bf16[256,512]{1,0:T(8,128)(2,1)S(1)}, bf16[256,512]{1,0:T(8,128)(2,1)S(1)}, u32[]{:S(2)}, u32[]{:S(2)}) collective-permute-start(bf16[256,512]{1,0:T(8,128)(2,1)S(1)} %collective-permute-done.43.refs_24_), channel_id=1, source_target_pairs={{0,4},{1,5},{2,6},{3,7},{4,8},{5,9},{6,10},{7,11},{8,12},{9,13},{1... | collective-permute-start | bytes 786440 | tf_op jit(solution)/shard_map/spread_differences/ppermute | solution.py:27
  250.5 11.3 %collective-permute-start.51 = (bf16[256,512]{1,0:T(8,128)(2,1)S(1)}, bf16[256,512]{1,0:T(8,128)(2,1)}, u32[]{:S(2)}, u32[]{:S(2)}) collective-permute-start(bf16[256,512]{1,0:T(8,128)(2,1)S(1)} %collective-permute-done.42.refs_23_), channel_id=1, source_target_pairs={{0,12},{1,13},{2,14},{3,15},{4,0},{5,1},{6,2},{7,3},{8,4},{9,5},{1... | collective-permute-start | bytes 786440 | tf_op jit(solution)/shard_map/spread_differences/ppermute | solution.py:27
  250.6 11.2 %collective-permute-start.50 = (bf16[256,512]{1,0:T(8,128)(2,1)S(1)}, bf16[256,512]{1,0:T(8,128)(2,1)S(1)}, u32[]{:S(2)}, u32[]{:S(2)}) collective-permute-start(bf16[256,512]{1,0:T(8,128)(2,1)S(1)} %collective-permute-done.42.refs_23_), channel_id=1, source_target_pairs={{0,4},{1,5},{2,6},{3,7},{4,8},{5,9},{6,10},{7,11},{8,12},{9,13},{1... | collective-permute-start | bytes 786440 | tf_op jit(solution)/shard_map/spread_differences/ppermute | solution.py:27
  256.1 9.4 %collective-permute-start.35 = (bf16[256,512]{1,0:T(8,128)(2,1)S(1)}, bf16[256,512]{1,0:T(8,128)(2,1)S(1)}, u32[]{:S(2)}, u32[]{:S(2)}) collective-permute-start(bf16[256,512]{1,0:T(8,128)(2,1)S(1)} %collective-permute-done.29.refs_12_), channel_id=1, source_target_pairs={{0,3},{1,0},{2,1},{3,2},{4,7},{5,4},{6,5},{7,6},{8,11},{9,8},{10,9... | collective-permute-start | bytes 786440 | tf_op jit(solution)/shard_map/spread_differences/ppermute | solution.py:27
  257.3 21.9 %collective-permute-start.34 = (bf16[512,512]{1,0:T(8,128)(2,1)}, bf16[512,512]{1,0:T(8,128)(2,1)}, u32[]{:S(2)}, u32[]{:S(2)}) collective-permute-start(bf16[512,512]{1,0:T(8,128)(2,1)} %collective-permute-done.26.refs_9_), channel_id=1, source_target_pairs={{0,1},{1,2},{2,3},{3,0},{4,5},{5,6},{6,7},{7,4},{8,9},{9,10},{10,1... | collective-permute-start | bytes 1572872 | tf_op jit(solution)/shard_map/spread_differences/ppermute | solution.py:27
  261.9 17.3 %collective-permute-start.33 = (bf16[512,512]{1,0:T(8,128)(2,1)}, bf16[512,512]{1,0:T(8,128)(2,1)}, u32[]{:S(2)}, u32[]{:S(2)}) collective-permute-start(bf16[512,512]{1,0:T(8,128)(2,1)} %collective-permute-done.25.refs_8_), channel_id=1, source_target_pairs={{0,3},{1,0},{2,1},{3,2},{4,7},{5,4},{6,5},{7,6},{8,11},{9,8},{10,9... | collective-permute-start | bytes 1572872 | tf_op jit(solution)/shard_map/spread_differences/ppermute | solution.py:27
  262.0 17.2 %collective-permute-start.56 = (bf16[512,512]{1,0:T(8,128)(2,1)}, bf16[512,512]{1,0:T(8,128)(2,1)}, u32[]{:S(2)}, u32[]{:S(2)}) collective-permute-start(bf16[512,512]{1,0:T(8,128)(2,1)} %collective-permute-done.48.refs_29_), channel_id=1, source_target_pairs={{0,4},{1,5},{2,6},{3,7},{4,8},{5,9},{6,10},{7,11},{8,12},{9,13},{1... | collective-permute-start | bytes 1572872 | tf_op jit(solution)/shard_map/spread_differences/ppermute | solution.py:27
  265.6 13.6 %collective-permute-start.55 = (bf16[512,512]{1,0:T(8,128)(2,1)}, bf16[512,512]{1,0:T(8,128)(2,1)}, u32[]{:S(2)}, u32[]{:S(2)}) collective-permute-start(bf16[512,512]{1,0:T(8,128)(2,1)} %collective-permute-done.47.refs_28_), channel_id=1, source_target_pairs={{0,12},{1,13},{2,14},{3,15},{4,0},{5,1},{6,2},{7,3},{8,4},{9,5},{1... | collective-permute-start | bytes 1572872 | tf_op jit(solution)/shard_map/spread_differences/ppermute | solution.py:27
  269.4 9.7 %collective-permute-start.57 = (bf16[256,512]{1,0:T(8,128)(2,1)}, bf16[256,512]{1,0:T(8,128)(2,1)}, u32[]{:S(2)}, u32[]{:S(2)}) collective-permute-start(bf16[256,512]{1,0:T(8,128)(2,1)} %collective-permute-done.51.refs_32_), channel_id=1, source_target_pairs={{0,12},{1,13},{2,14},{3,15},{4,0},{5,1},{6,2},{7,3},{8,4},{9,5},{1... | collective-permute-start | bytes 786440 | tf_op jit(solution)/shard_map/spread_differences/ppermute | solution.py:27
  (55 other events, 1632.8 us)
